TPU v7x, 32 devices: a whole 2x2x4 slice. The times are simulated.
32 devices in a mesh: chan: 8 (over z, x), hour: 4 (over y, core).
Axes of the slice: x: 2, y: 2, z: 4, core: 2. Of those that a mesh axis runs over, the one named last changes fastest.
Arguments:
- traces: bfloat16 [1024, 16384], P('chan', 'hour'), may hold values from -6 to 6
- taps: bfloat16 [1024, 512], P('chan'), may hold values from -0.25 to 0.25
- bin_ids: int32 [4, 8], P(None, 'chan'), may hold values from 0 to 31
- owners: int32 [32], replicated, may hold values from 0 to 31, each once
Outputs:
- stacks: float32 [32, 8192], P(('chan', 'hour'))
Inputs may be any that keep to these rules, and one draw needn't show every extreme that they name: bin_ids[r, i] is the distance bin of the pair of block i - r - 1 with block i; entries with i <= r name no pair and are not read. owners is a permutation: bin b is held in row owners[b] of stacks.
All inputs are finite; a program needn't handle non-finite values.
Results may differ from a plain program's by a relative error of at most 0.004.
Values may be sent and summed in bfloat16 or wider, within the bound.
A program may use at most 256 MiB of HBM per device.

v0:
```python
import functools
import math

import jax
import jax.numpy as jnp
import numpy as np
from jax import lax
from jax.experimental import pallas as pl
from jax.experimental.pallas import tpu as pltpu
from jax.sharding import PartitionSpec as P

FR = 4096
ROUNDS = 4
MESH = pl.DeviceIdType.MESH


exact = lax.Precision.HIGHEST

def passed_along(shard, axis, by):
    devices = lax.axis_size(axis)
    pairs = [(i, i + by) for i in range(devices) if 0 <= i + by < devices]
    return lax.ppermute(shard, axis, pairs)


def transform(real_part, imag_part, count):
    span = real_part.shape[-1]
    inner = 2 * span // 128
    lead = real_part.shape[:-1]
    first = jnp.arange(64, dtype=jnp.float32)[:, None]
    middle = jnp.arange(128, dtype=jnp.float32)[None, :]
    angle_one = 2.0 * math.pi / 128.0 * jnp.mod(first * middle, 128.0)
    cos_one = jnp.cos(angle_one)
    sin_one = -jnp.sin(angle_one)
    second = jnp.arange(inner, dtype=jnp.float32)[:, None]
    angle_turn = 2.0 * math.pi / (128.0 * inner) * jnp.mod(second * middle, 128.0 * inner)
    cos_turn = jnp.cos(angle_turn)
    sin_turn = -jnp.sin(angle_turn)
    outer = jnp.arange(count // 128, dtype=jnp.float32)[None, :]
    angle_two = 2.0 * math.pi / inner * jnp.mod(second * outer, float(inner))
    cos_two = jnp.cos(angle_two)
    sin_two = -jnp.sin(angle_two)
    grid = real_part.reshape(lead + (64, inner))
    section_re = jnp.einsum("...an,ak->...nk", grid, cos_one, precision=exact)
    section_im = jnp.einsum("...an,ak->...nk", grid, sin_one, precision=exact)
    if imag_part is not None:
        grid_im = imag_part.reshape(lead + (64, inner))
        section_re = section_re - jnp.einsum("...an,ak->...nk", grid_im, sin_one, precision=exact)
        section_im = section_im + jnp.einsum("...an,ak->...nk", grid_im, cos_one, precision=exact)
    turned_re = section_re * cos_turn - section_im * sin_turn
    turned_im = section_re * sin_turn + section_im * cos_turn
    out_re = jnp.einsum("...nk,nm->...mk", turned_re, cos_two, precision=exact) - jnp.einsum(
        "...nk,nm->...mk", turned_im, sin_two, precision=exact
    )
    out_im = jnp.einsum("...nk,nm->...mk", turned_re, sin_two, precision=exact) + jnp.einsum(
        "...nk,nm->...mk", turned_im, cos_two, precision=exact
    )
    return (out_re.reshape(lead + (count,)), out_im.reshape(lead + (count,)))


def filtered(samples, filters):
    channels = samples.shape[0]
    frames = samples.shape[1] // FR
    signal = samples.astype(jnp.float32).reshape(channels, frames, FR)
    freq_re, freq_im = transform(signal, None, FR)
    padded_taps = jnp.pad(filters.astype(jnp.float32), ((0, 0), (0, FR - filters.shape[1])))
    resp_re, resp_im = transform(padded_taps, None, FR)
    resp_re = resp_re[:, None, :]
    resp_im = resp_im[:, None, :]
    spec_re = (freq_re * resp_re - freq_im * resp_im).astype(jnp.bfloat16)
    spec_im = (freq_re * resp_im + freq_im * resp_re).astype(jnp.bfloat16)
    return (spec_re, spec_im)


def body(traces, taps, bin_ids, owners):
    channels = traces.shape[0]
    frames = traces.shape[1] // FR
    spec_re, spec_im = filtered(traces, taps)
    mine = lax.axis_index("chan")
    near_re = spec_re.astype(jnp.float32)
    near_im = spec_im.astype(jnp.float32)
    results = []
    for offset in range(ROUNDS):
        far_re, far_im = passed_along((spec_re, spec_im), "chan", offset + 1)
        far_re = far_re.astype(jnp.float32)
        far_im = far_im.astype(jnp.float32)
        cross_re = jnp.sum(far_re * near_re + far_im * near_im, axis=(0, 1))
        cross_im = jnp.sum(far_im * near_re - far_re * near_im, axis=(0, 1))
        results.append(jnp.stack([cross_re, cross_im]))
    contrib = jnp.stack(results)
    nbins = owners.shape[0]
    own_bins = bin_ids[:, 0]
    labels = jnp.arange(nbins, dtype=jnp.int32)
    places = jnp.sum(jnp.where(own_bins[:, None] == labels[None, :], owners[None, :], 0), axis=1)
    valid = jnp.arange(ROUNDS, dtype=jnp.int32) < mine
    places = jnp.where(valid, places, -1)
    width = contrib.shape[2]
    flat = contrib.reshape(ROUNDS, 2 * width)
    per_device = nbins // lax.axis_size("chan")
    rows = jnp.arange(lax.axis_size("chan") * per_device, dtype=jnp.int32)
    onehot = (places[None, :] == rows[:, None]).astype(jnp.float32)
    stacked = lax.psum_scatter(
        jnp.dot(onehot, flat, precision=exact, preferred_element_type=jnp.float32),
        "chan",
        scatter_dimension=0,
        tiled=True,
    )
    stacked = stacked.reshape(per_device, 2, width)
    final = lax.psum_scatter(stacked, "hour", scatter_dimension=0, tiled=True)
    weights = jnp.where(jnp.arange(FR) == 0, 1.0, 2.0).astype(jnp.float32)
    wave_re, wave_im = transform(final[:, 0] * weights, -final[:, 1] * weights, 2 * FR)
    norm = 1.0 / (FR * math.sqrt(FR * lax.axis_size("hour") * frames * channels))
    return wave_re * norm

SPLIT = 8
SUB = FR // SPLIT
LANES = 128
TILES = SUB // LANES


def sub_tables():
    a = np.arange(SUB)[:, None]
    k1 = np.arange(SUB)[None, :]
    turn = 2.0 * np.pi * ((a * k1) % (2 * SUB)) / (2 * SUB)
    cos, sin = np.cos(turn), -np.sin(turn)
    sin[:, 0] = 1.0 - 2.0 * (np.arange(SUB) % 2)
    table = np.stack([cos.reshape(SUB, TILES, LANES), sin.reshape(SUB, TILES, LANES)], axis=2)
    return table.reshape(SUB, 2 * SUB)


def two_parts(table):
    high = table.astype(jnp.bfloat16)
    low = (table - high.astype(np.float64)).astype(jnp.bfloat16)
    return high, low


def pick_table():
    span = SPLIT * LANES
    table = np.zeros((span, span), np.float32)
    for n in range(SPLIT):
        for b in range(LANES):
            table[SPLIT * b + n, n * LANES + b] = 1.0
    return table.astype(jnp.bfloat16)


def turn_table():
    n = np.arange(SPLIT)[:, None]
    k1 = np.arange(SUB)[None, :]
    turn = 2.0 * np.pi * n * k1 / (2 * FR)
    table = np.stack([np.cos(turn), -np.sin(turn)], axis=1).reshape(SPLIT, 2, TILES, 1, LANES)
    table = np.broadcast_to(table.transpose(2, 0, 1, 3, 4), (TILES, SPLIT, 2, 8, LANES))
    return np.ascontiguousarray(table).astype(np.float32)


def times(value, angle):
    re, im = value
    c, s = math.cos(angle), math.sin(angle)
    if abs(s) < 1e-12:
        return (re, im) if c > 0 else (-re, -im)
    if abs(c) < 1e-12:
        return (-im, re) if s > 0 else (im, -re)
    if abs(abs(c) - abs(s)) < 1e-12:
        root = abs(c)
        p, q = math.copysign(1.0, c), math.copysign(1.0, s)
        first = (re if p > 0 else -re) + (-im if q > 0 else im)
        second = (re if q > 0 else -re) + (im if p > 0 else -im)
        return first * root, second * root
    return re * c - im * s, re * s + im * c


def small_dft(values, sign, half=False):
    size = len(values)
    if size == 1:
        return values
    even = small_dft(values[0::2], sign)
    odd = small_dft(values[1::2], sign)
    low, high = [], []
    for k in range(size // 2):
        turned = times(odd[k], sign * 2.0 * math.pi * k / size)
        low.append((even[k][0] + turned[0], even[k][1] + turned[1]))
        if not half:
            high.append((even[k][0] - turned[0], even[k][1] - turned[1]))
    return low + high


def pairs_of(blocks):
    return [(r, i) for r in range(ROUNDS) for i in range(blocks) if i >= r + 1]


def rows_of_pairs(ids, owners, chan, hour):
    depth = ids.shape[1]
    nbins = owners.shape[1]
    bins = lax.broadcasted_iota(jnp.int32, (nbins, depth), 0) + 1
    picked = (bins == ids[0:1, :]).astype(jnp.float32).astype(jnp.bfloat16)
    place = lax.broadcasted_iota(jnp.int32, (nbins, nbins), 0)
    row = lax.rem(place, chan) * hour + lax.div(place, chan)
    moved = (row == owners[...]).astype(jnp.float32).astype(jnp.bfloat16)
    return jnp.dot(moved, picked, preferred_element_type=jnp.float32).astype(jnp.bfloat16)


def mix_table():
    l2 = np.arange(SPLIT)[None, :]
    k2 = np.arange(SPLIT)[:, None]
    main = 2.0 * np.pi * k2 * l2 / SPLIT
    extra = 2.0 * np.pi * ((k2 - SPLIT // 2) * l2 / SPLIT + l2 / (2 * SPLIT))
    table = np.stack([np.cos(main), np.sin(main), np.cos(extra), np.sin(extra)])
    return np.ascontiguousarray(np.broadcast_to(table[..., None], (4, SPLIT, SPLIT, LANES))).astype(np.float32)


def back_table():
    l2 = np.arange(SPLIT)[:, None]
    turn = 2.0 * np.pi * l2 * np.arange(SUB)[None, :] / (2 * FR)
    table = np.stack([np.cos(turn), np.sin(turn)]).reshape(2, SPLIT, TILES, LANES)
    return np.ascontiguousarray(table.transpose(2, 0, 1, 3)).astype(np.float32)


def over_lanes(a, b):
    return lax.dot_general(a, b, (((1,), (1,)), ((), ())), preferred_element_type=jnp.float32)


def inverse(row, mix, back, high, low, norm):
    lane = lax.broadcasted_iota(jnp.int32, (SPLIT, LANES), 1)
    slot = lax.broadcasted_iota(jnp.int32, (SPLIT, LANES), 0)
    plain, flipped = [], []
    for t in range(TILES):
        re = row[t * SPLIT : (t + 1) * SPLIT, :LANES] * (2.0 * norm)
        im = row[t * SPLIT : (t + 1) * SPLIT, LANES:] * (2.0 * norm)
        main_re, main_im = re, im
        if t == 0:
            main_re = jnp.where(lane == 0, jnp.where(slot == 0, re * 0.5, re), re)
            drop = (lane == 0) & (slot >= SPLIT // 2)
            main_re = jnp.where(drop, 0.0, main_re)
            main_im = jnp.where(drop, 0.0, im)
        g_re = g_im = jnp.zeros((SPLIT, LANES), jnp.float32)
        for k2 in range(SPLIT):
            a, b = main_re[k2 : k2 + 1, :], main_im[k2 : k2 + 1, :]
            c, s = mix[0, k2], mix[1, k2]
            g_re = g_re + (c * a - s * b)
            g_im = g_im + (s * a + c * b)
        c, s = back[t, 0], back[t, 1]
        y_re, y_im = g_re * c - g_im * s, g_re * s + g_im * c
        if t == 0:
            more = jnp.zeros((SPLIT, LANES), jnp.float32)
            for k2 in range(SPLIT // 2, SPLIT):
                more = more + (mix[2, k2] * re[k2 : k2 + 1, :] - mix[3, k2] * im[k2 : k2 + 1, :])
            y_im = jnp.where(lane == 0, more, y_im)
        sign = jnp.where(lax.rem(lane, 2) == 0, 1.0, -1.0)
        plain += [y_re, y_im]
        flipped += [y_re * sign, y_im * sign]
    y = jnp.concatenate([jnp.concatenate(plain, axis=1), jnp.concatenate(flipped, axis=1)], axis=0)
    top = y.astype(jnp.bfloat16)
    rest = (y - top.astype(jnp.float32)).astype(jnp.bfloat16)
    return over_lanes(top, high[...]) + (over_lanes(rest, high[...]) + over_lanes(top, low[...]))


def kernel(chan, hour, norm, x, taps, bin_ids, owners, *refs):
    tables, out = refs[:6], refs[6]
    held = refs[7:13]
    pick, high, low, turns, mix, back = held
    xin, tin, ids, ids_in, xd, td, fx, fh, spec, cross, part, first, sums, second = refs[13:27]
    table_sem, own_sem, ids_send, ids_recv, t_send, t_recv, x_send, x_recv = refs[27:35]
    f_send, f_recv, send, recv, send2, recv2 = refs[35:]
    me, my_hour = lax.axis_index("chan"), lax.axis_index("hour")
    per = xin.shape[1]
    span = SPLIT * LANES
    share = pl.ds(pl.multiple_of(my_hour * (tin.shape[2] // hour), LANES), tin.shape[2] // hour)

    def partner(o):
        to, bit = me, 1
        while bit < chan:
            to = to + lax.rem(lax.div(o, bit), 2) * bit * (1 - 2 * lax.rem(lax.div(me, bit), 2))
            bit *= 2
        return to

    def sent(src, dst, sends, recvs, **device):
        return pltpu.make_async_remote_copy(
            src_ref=src, dst_ref=dst, send_sem=sends, recv_sem=recvs, device_id=device, device_id_type=MESH
        )

    loads = [pltpu.make_async_copy(src, dst, table_sem.at[z]) for z, (src, dst) in enumerate(zip(tables, held))]
    own = [
        pltpu.make_async_copy(x.at[me], xin.at[me], own_sem.at[0]),
        pltpu.make_async_copy(taps.at[me, :, share], tin.at[me, :, share], own_sem.at[1]),
    ]
    for copy in own + loads:
        copy.start()
    barrier = pltpu.get_barrier_semaphore()
    for o in range(1, hour):
        pl.semaphore_signal(
            barrier, inc=1, device_id={"hour": lax.rem(my_hour + o, hour)}, device_id_type=MESH
        )
    for o in range(1, chan):
        pl.semaphore_signal(barrier, inc=1, device_id={"chan": partner(o)}, device_id_type=MESH)
    place = lax.div(lax.broadcasted_iota(jnp.int32, ids.shape, 1), 8)
    labels = jnp.zeros(ids.shape, jnp.int32)
    for r in range(ROUNDS):
        live = (place == me * ROUNDS + r) & (me >= r + 1)
        labels = jnp.where(live, bin_ids[:, r : r + 1] + 1, labels)
    ids[...] = labels
    pl.semaphore_wait(barrier, chan + hour - 2)

    def x_copy(o):
        to = partner(o)
        return sent(x.at[to], xin.at[me], x_send.at[o], x_recv.at[o], chan=to)

    far_first = sorted(range(1, chan), key=lambda o: -(o.bit_length()))
    tap_copies, id_copies = [], []
    for o in far_first:
        to = partner(o)
        tap_copies.append(
            sent(taps.at[to, :, share], tin.at[me, :, share], t_send.at[o], t_recv.at[o], chan=to)
        )
        tap_copies[-1].start()
    for o in far_first:
        id_copies.append(sent(ids, ids_in.at[o], ids_send.at[o], ids_recv.at[o], chan=partner(o)))
        id_copies[-1].start()
    for o in range(1, chan):
        x_copy(o).start()
    own[1].wait()
    for copy in tap_copies:
        copy.wait_recv()
    forwards = []
    for o in range(1, hour):
        to = lax.rem(my_hour + o, hour)
        forwards.append(sent(tin.at[:, :, share], tin.at[:, :, share], f_send.at[o], f_recv.at[o], hour=to))
        forwards[-1].start()
    for copy in loads + own[:1]:
        copy.wait()

    lane0 = lax.broadcasted_iota(jnp.int32, (8, LANES), 1) == 0

    def spectra(block, t, edge):
        @pl.loop(0, per // 8)
        def _(g):
            piece = pl.ds(pl.multiple_of(8 * g, 8), 8)
            here = pl.ds(pl.multiple_of(block * per + 8 * g, 8), 8)

            def bins_of(f, rows):
                values, extra = [], []
                for n in range(SPLIT):
                    re = f[n, rows, pl.ds(pl.multiple_of(2 * t * LANES, LANES), LANES)]
                    im = f[n, rows, pl.ds(pl.multiple_of((2 * t + 1) * LANES, LANES), LANES)]
                    if edge:
                        angle = -math.pi * n / SPLIT
                        extra.append((im * math.cos(angle), im * math.sin(angle)))
                        im = jnp.where(lane0, 0.0, im)
                    if n == 0:
                        values.append((re, im))
                    else:
                        c, s = turns[t, n, 0], turns[t, n, 1]
                        values.append((re * c - im * s, re * s + im * c))
                found = small_dft(values, -1)
                if edge:
                    more = small_dft(extra, -1, half=True)
                    for k2 in range(SPLIT // 2):
                        old = found[SPLIT // 2 + k2]
                        found[SPLIT // 2 + k2] = tuple(
                            jnp.where(lane0, more[k2][z], old[z]) for z in range(2)
                        )
                return found

            freq = bins_of(fx, piece)
            resp = bins_of(fh, here)
            for k2 in range(SPLIT):
                (xr, xi), (hr, hi) = freq[k2], resp[k2]
                spec[t, k2, 0, here, :] = (xr * hr - xi * hi).astype(jnp.bfloat16).astype(jnp.float32)
                spec[t, k2, 1, here, :] = (xr * hi + xi * hr).astype(jnp.bfloat16).astype(jnp.float32)

    def take(block):
        flat = jnp.concatenate([xin[block, :, q * span : (q + 1) * span] for q in range(FR // span)], axis=0)
        got = jnp.dot(flat, pick[...], preferred_element_type=jnp.float32).astype(jnp.bfloat16)
        for q in range(FR // span):
            for n in range(SPLIT):
                xd[n * per : (n + 1) * per, q * LANES : (q + 1) * LANES] = got[
                    q * per : (q + 1) * per, n * LANES : (n + 1) * LANES
                ]
        found = jnp.dot(xd[...], high[...], preferred_element_type=jnp.float32) + jnp.dot(
            xd[...], low[...], preferred_element_type=jnp.float32
        )
        for n in range(SPLIT):
            fx[n] = found[n * per : (n + 1) * per]
        spectra(block, 0, True)

        @pl.loop(1, TILES)
        def _(t):
            spectra(block, t, False)

    for copy in forwards:
        copy.wait_recv()
    count = tin.shape[2]
    got = jnp.dot(
        tin[...].reshape(chan * per, count), pick[:count, :], preferred_element_type=jnp.float32
    ).astype(jnp.bfloat16)
    for n in range(SPLIT):
        td[n] = got[:, n * LANES : (n + 1) * LANES]

    @pl.loop(0, SPLIT)
    def _(n):
        fh[n] = jnp.dot(td[n], high[:LANES, :], preferred_element_type=jnp.float32) + jnp.dot(
            td[n], low[:LANES, :], preferred_element_type=jnp.float32
        )

    for copy in id_copies:
        copy.wait_recv()
    labels = ids[...]
    for o in range(1, chan):
        labels = labels + ids_in[o]
    onehot = rows_of_pairs(labels, owners, chan, hour)
    cross[...] = jnp.zeros_like(cross)

    take(me)

    @pl.loop(1, chan // 2)
    def _(o):
        x_copy(o).wait_recv()
        take(partner(o))

    @pl.loop(chan // 2, chan)
    def _(o):
        x_copy(o).wait_recv()
        take(partner(o))

    pairs = pairs_of(chan)
    steps = SPLIT // 2

    def part_copy(t, o):
        to = lax.rem(my_hour + o, hour)
        where = pl.ds(t * steps, steps)
        return sent(part.at[to, where], first.at[o, where], send.at[t, o], recv.at[t, o], hour=to)

    @pl.loop(0, TILES)
    def _(t):
        @pl.loop(0, steps)
        def _(kk):
            both = []
            for e in range(2):
                k2 = 2 * kk + e
                for r, i in pairs:
                    p = i * ROUNDS + r
                    re = im = None
                    for c in range(per // 8):
                        near = pl.ds(i * per + 8 * c, 8)
                        far = pl.ds((i - r - 1) * per + 8 * c, 8)
                        nr, ni = spec[t, k2, 0, near, :], spec[t, k2, 1, near, :]
                        fr, fi = spec[t, k2, 0, far, :], spec[t, k2, 1, far, :]
                        one, two = fr * nr + fi * ni, fi * nr - fr * ni
                        re, im = (one, two) if re is None else (re + one, im + two)
                    cross[8 * p : 8 * p + 8, :LANES] = re
                    cross[8 * p : 8 * p + 8, LANES:] = im
                total = cross[...]
                top = total.astype(jnp.bfloat16)
                rest = (total - top.astype(jnp.float32)).astype(jnp.bfloat16)
                both.append(
                    jnp.dot(onehot, top, preferred_element_type=jnp.float32)
                    + jnp.dot(onehot, rest, preferred_element_type=jnp.float32)
                )
            for h in range(hour):
                rows_of = slice(h * chan, (h + 1) * chan)
                part[h, t * steps + kk] = jnp.concatenate(
                    [both[0][rows_of], both[1][rows_of]], axis=0
                ).astype(jnp.bfloat16)

        for o in range(1, hour):
            part_copy(t, o).start()

    width = 2 * LANES
    depth = chan * TILES * SPLIT
    for t in range(TILES):
        for o in range(1, hour):
            part_copy(t, o).wait_recv()
    total = part[my_hour].astype(jnp.float32)
    for o in range(1, hour):
        total = total + first[o].astype(jnp.float32)
    total = total.reshape(depth, width).astype(jnp.bfloat16)
    to_row = lax.broadcasted_iota(jnp.int32, (depth, depth), 0)
    from_row = lax.broadcasted_iota(jnp.int32, (depth, depth), 1)
    slots = TILES * SPLIT
    wanted = lax.rem(to_row, slots) * chan + lax.div(to_row, slots)
    swap = (wanted == from_row).astype(jnp.float32).astype(jnp.bfloat16)
    sums[...] = jnp.dot(swap, total, preferred_element_type=jnp.float32).astype(jnp.bfloat16).reshape(sums.shape)
    later = []
    for o in far_first:
        to = partner(o)
        later.append(sent(sums.at[to], second.at[o], send2.at[o], recv2.at[o], chan=to))
        later[-1].start()
    row = sums[me].astype(jnp.float32)
    for copy in later:
        copy.wait_recv()
    for o in range(1, chan):
        row = row + second[o].astype(jnp.float32)
    out[...] = inverse(row, mix, back, high, low, norm)
    for copy in tap_copies + id_copies + forwards + later:
        copy.wait_send()
    for o in range(1, chan):
        x_copy(o).wait_send()
    for t in range(TILES):
        for o in range(1, hour):
            part_copy(t, o).wait_send()


def split_body(traces, taps, bin_ids, owners):
    chan, hour = lax.axis_size("chan"), lax.axis_size("hour")
    channels, count = taps.shape
    per = channels // chan
    norm = 1.0 / (FR * math.sqrt(FR * hour * channels))
    high, low = two_parts(sub_tables())
    tables = [pick_table(), high, low, turn_table(), mix_table(), back_table()]
    depth = 8 * ROUNDS * chan
    slots = TILES * SPLIT
    part = (hour, slots // 2, 2 * chan, 2 * LANES)
    sums = (chan, slots, 2 * LANES)
    vmem, hbm = pl.BlockSpec(memory_space=pltpu.VMEM), pl.BlockSpec(memory_space=pl.ANY)
    sems = pltpu.SemaphoreType.DMA
    wave = pl.pallas_call(
        functools.partial(kernel, chan, hour, norm),
        out_shape=jax.ShapeDtypeStruct((2 * SPLIT, SUB), jnp.float32),
        in_specs=[hbm, hbm, vmem, vmem] + [hbm] * len(tables),
        out_specs=vmem,
        scratch_shapes=[pltpu.VMEM(table.shape, table.dtype) for table in tables]
        + [
            pltpu.VMEM((chan, per, FR), jnp.bfloat16),
            pltpu.VMEM((chan, per, count), jnp.bfloat16),
            pltpu.VMEM((8, depth), jnp.int32),
            pltpu.VMEM((chan, 8, depth), jnp.int32),
            pltpu.VMEM((SPLIT * per, SUB), jnp.bfloat16),
            pltpu.VMEM((SPLIT, channels, LANES), jnp.bfloat16),
            pltpu.VMEM((SPLIT, per, 2 * SUB), jnp.float32),
            pltpu.VMEM((SPLIT, channels, 2 * SUB), jnp.float32),
            pltpu.VMEM((TILES, SPLIT, 2, channels, LANES), jnp.float32),
            pltpu.VMEM((depth, 2 * LANES), jnp.float32),
            pltpu.VMEM(part, jnp.bfloat16),
            pltpu.VMEM(part, jnp.bfloat16),
            pltpu.VMEM(sums, jnp.bfloat16),
            pltpu.VMEM(sums, jnp.bfloat16),
            sems((len(tables),)),
            sems((2,)),
        ]
        + [sems((chan,))] * 6
        + [sems((hour,))] * 2
        + [sems((TILES, hour))] * 2
        + [sems((chan,))] * 2,
        compiler_params=pltpu.CompilerParams(
            collective_id=0, has_side_effects=True, vmem_limit_bytes=56 * 2**20
        ),
    )(
        traces.reshape(chan, per, FR),
        taps.reshape(chan, per, count),
        bin_ids.T,
        owners.reshape(1, -1),
        *[jnp.asarray(table) for table in tables],
    )
    return wave.reshape(2, SPLIT, SUB).transpose(0, 2, 1).reshape(1, 2 * FR)


def solution(mesh):
    placed = (P("chan", "hour"), P("chan", None), P(None, "chan"), P())

    def whole(traces, taps, bin_ids, owners):
        chan, hour = mesh.shape["chan"], mesh.shape["hour"]
        channels = traces.shape[0] // chan
        fits = (
            chan == 8
            and channels % (16 * chan) == 0
            and traces.shape[1] == hour * FR
            and taps.shape[1] == SPLIT * LANES // 2
            and owners.shape[0] == chan * hour
        )
        return jax.shard_map(
            split_body if fits else body,
            mesh=mesh,
            in_specs=placed,
            out_specs=P(("chan", "hour"), None),
            check_vma=False,
        )(traces, taps, bin_ids, owners)

    return whole
```

profile of v0, /device:TPU:0, one launch (start us, length us, event | category | flops | bytes accessed | tf_op | source)
XLA Modules:
  0.0 51.6 jit_solution(8806901127407343985)
XLA Ops:
  0.0 49.7 %shard_map.100 = f32[16,512]{1,0:T(8,128)} custom-call(bf16[8,16,4096]{2,1,0:T(8,128)(2,1)} %bitcast.7, bf16[8,16,512]{2,1,0:T(8,128)(2,1)} %bitcast.9, s32[1,4]{1,0:T(1,128)} %bitcast.10, s32[1,32]{1,0:T(1,128)} %bitcast.11, bf16[1024,1024]{1,0:T(8,128)(2,1)} %constant.12.clone.refs_0_, bf16[512,1024]{1,0:T(8,128)(2,1)} %constant.13.clone.refs_1_, ...), custom_call_target="tpu_custom_call" | custom-call | tf_op jit(solution)/shard_map/pallas_call | solution.py:513
  49.8 1.0 %copy.12 = f32[2,8,512]{1,2,0:T(8,128)S(1)} copy(f32[2,8,512]{2,1,0:T(8,128)} %bitcast.8) | data formatting | bytes 65536 | tf_op jit(solution)/shard_map/reshape | solution.py:551
  50.7 0.9 %reshape.19 = f32[1,8192]{1,0:T(1,128)} reshape(f32[2,512,8]{2,1,0:T(8,128)S(1)} %bitcast.6) | data formatting | bytes 65536 | tf_op jit(solution)/shard_map/reshape | solution.py:551
where the time goes:
time: 51.8 us; the launch traced here: 51.6 us
  Pallas kernels  49.7 us (96%)
  local copies, waits for them, and re-layouts  1.86 us (4%)
    pallas_call x1, Pallas kernels, split_body(): pl.pallas_call(functools.partial(kernel, chan, hour, norm), out_shape=jax...  49.7 us
    reshape x2, local copies, waits for them, and re-layouts, split_body(): return wave.reshape(2, SPLIT, SUB).transpose(0, 2, 1).reshape(1, 2 * FR)  1.86 us

commit v1 on v0

--- a/solution.py
+++ b/solution.py
@@ -182,94 +182,121 @@
     return low + high
 
 
-def pairs_of(blocks):
-    return [(r, i) for r in range(ROUNDS) for i in range(blocks) if i >= r + 1]
-
-
-def rows_of_pairs(ids, owners, chan, hour):
+LATE = 8
+SLOTS = 32
+
+
+def slot_of(step, before, chan):
+    if isinstance(step, int) and step == chan - 1:
+        return before
+    return LATE + step * (step - 1) // 2 + before
+
+
+def rows_of_pairs(ids, owners):
     depth = ids.shape[1]
     nbins = owners.shape[1]
     bins = lax.broadcasted_iota(jnp.int32, (nbins, depth), 0) + 1
     picked = (bins == ids[0:1, :]).astype(jnp.float32).astype(jnp.bfloat16)
-    place = lax.broadcasted_iota(jnp.int32, (nbins, nbins), 0)
-    row = lax.rem(place, chan) * hour + lax.div(place, chan)
+    row = lax.broadcasted_iota(jnp.int32, (nbins, nbins), 0)
     moved = (row == owners[...]).astype(jnp.float32).astype(jnp.bfloat16)
     return jnp.dot(moved, picked, preferred_element_type=jnp.float32).astype(jnp.bfloat16)
 
 
-def mix_table():
-    l2 = np.arange(SPLIT)[None, :]
-    k2 = np.arange(SPLIT)[:, None]
-    main = 2.0 * np.pi * k2 * l2 / SPLIT
-    extra = 2.0 * np.pi * ((k2 - SPLIT // 2) * l2 / SPLIT + l2 / (2 * SPLIT))
-    table = np.stack([np.cos(main), np.sin(main), np.cos(extra), np.sin(extra)])
-    return np.ascontiguousarray(np.broadcast_to(table[..., None], (4, SPLIT, SPLIT, LANES))).astype(np.float32)
-
-
-def back_table():
-    l2 = np.arange(SPLIT)[:, None]
-    turn = 2.0 * np.pi * l2 * np.arange(SUB)[None, :] / (2 * FR)
-    table = np.stack([np.cos(turn), np.sin(turn)]).reshape(2, SPLIT, TILES, LANES)
-    return np.ascontiguousarray(table.transpose(2, 0, 1, 3)).astype(np.float32)
+def fold(values):
+    sublane = lax.broadcasted_iota(jnp.int32, values[0].shape, 0)
+    shift = 1
+    while len(values) > 1:
+        first = lax.rem(lax.div(sublane, shift), 2) == 0
+        values = [
+            jnp.where(first, a, b) + pltpu.roll(jnp.where(first, b, a), SPLIT - shift, 0)
+            for a, b in zip(values[0::2], values[1::2])
+        ]
+        shift *= 2
+    return values[0]
+
+
+OUT_ROWS = 2 * FR // LANES
+TERMS = 2 * SPLIT * (TILES + 1)
+
+
+def column_table():
+    v = np.arange(LANES)[:, None]
+    t, k2 = np.arange(TILES)[None, :, None], np.arange(SPLIT)[None, None, :]
+    main = 2.0 * np.pi * ((v[:, :, None] * (SPLIT * k2 + t)) % OUT_ROWS) / OUT_ROWS
+    extra = 2.0 * np.pi * ((v * (SPLIT // 2 + SPLIT * (np.arange(SPLIT)[None, :] - SPLIT // 2))) % OUT_ROWS) / OUT_ROWS
+    phase = np.concatenate([main, extra[:, None, :]], axis=1)
+    top = np.stack([np.cos(phase), -np.sin(phase)], axis=2).reshape(LANES, TERMS)
+    under = np.stack([np.sin(phase), np.cos(phase)], axis=2).reshape(LANES, TERMS)
+    high, low = two_parts(np.concatenate([top, under], axis=0))
+    rest = np.zeros((2 * LANES, 2 * LANES - 3 * TERMS), jnp.bfloat16)
+    return np.concatenate([high, high, low, rest], axis=1)
+
+
+def twist_table():
+    turn = 2.0 * np.pi * np.arange(LANES)[:, None] * np.arange(LANES)[None, :] / (2 * FR)
+    return np.stack([np.cos(turn), np.sin(turn)]).astype(np.float32)
+
+
+def row_table():
+    turn = 2.0 * np.pi * ((np.arange(OUT_ROWS)[:, None] * np.arange(LANES)[None, :]) % OUT_ROWS) / OUT_ROWS
+    high, low = two_parts(np.concatenate([np.cos(turn), -np.sin(turn)], axis=1))
+    return np.concatenate([high, high, low], axis=1)
+
+
+def halves(value):
+    top = value.astype(jnp.bfloat16)
+    return top, (value - top.astype(jnp.float32)).astype(jnp.bfloat16)
 
 
 def over_lanes(a, b):
     return lax.dot_general(a, b, (((1,), (1,)), ((), ())), preferred_element_type=jnp.float32)
 
 
-def inverse(row, mix, back, high, low, norm):
-    lane = lax.broadcasted_iota(jnp.int32, (SPLIT, LANES), 1)
-    slot = lax.broadcasted_iota(jnp.int32, (SPLIT, LANES), 0)
-    plain, flipped = [], []
-    for t in range(TILES):
-        re = row[t * SPLIT : (t + 1) * SPLIT, :LANES] * (2.0 * norm)
-        im = row[t * SPLIT : (t + 1) * SPLIT, LANES:] * (2.0 * norm)
-        main_re, main_im = re, im
-        if t == 0:
-            main_re = jnp.where(lane == 0, jnp.where(slot == 0, re * 0.5, re), re)
-            drop = (lane == 0) & (slot >= SPLIT // 2)
-            main_re = jnp.where(drop, 0.0, main_re)
-            main_im = jnp.where(drop, 0.0, im)
-        g_re = g_im = jnp.zeros((SPLIT, LANES), jnp.float32)
-        for k2 in range(SPLIT):
-            a, b = main_re[k2 : k2 + 1, :], main_im[k2 : k2 + 1, :]
-            c, s = mix[0, k2], mix[1, k2]
-            g_re = g_re + (c * a - s * b)
-            g_im = g_im + (s * a + c * b)
-        c, s = back[t, 0], back[t, 1]
-        y_re, y_im = g_re * c - g_im * s, g_re * s + g_im * c
-        if t == 0:
-            more = jnp.zeros((SPLIT, LANES), jnp.float32)
-            for k2 in range(SPLIT // 2, SPLIT):
-                more = more + (mix[2, k2] * re[k2 : k2 + 1, :] - mix[3, k2] * im[k2 : k2 + 1, :])
-            y_im = jnp.where(lane == 0, more, y_im)
-        sign = jnp.where(lax.rem(lane, 2) == 0, 1.0, -1.0)
-        plain += [y_re, y_im]
-        flipped += [y_re * sign, y_im * sign]
-    y = jnp.concatenate([jnp.concatenate(plain, axis=1), jnp.concatenate(flipped, axis=1)], axis=0)
-    top = y.astype(jnp.bfloat16)
-    rest = (y - top.astype(jnp.float32)).astype(jnp.bfloat16)
-    return over_lanes(top, high[...]) + (over_lanes(rest, high[...]) + over_lanes(top, low[...]))
+def inverse(rows, column, twist, across, norm):
+    lane = lax.broadcasted_iota(jnp.int32, rows.shape, 1)
+    slot = lax.broadcasted_iota(jnp.int32, rows.shape, 0)
+    rows = rows * jnp.where((lane == 0) & (slot == 0), norm, 2.0 * norm)
+    apart = (lane == 0) & (slot < 2 * SPLIT) & (lax.rem(slot, SPLIT) >= SPLIT // 2)
+    every = jnp.concatenate(
+        [jnp.where(apart, 0.0, rows), jnp.where(apart, rows, 0.0)[: 2 * SPLIT]], axis=0
+    )
+    top, rest = halves(every)
+    nothing = jnp.zeros((2 * LANES - 3 * TERMS, LANES), jnp.bfloat16)
+    z = jnp.dot(
+        column[...], jnp.concatenate([top, rest, top, nothing], axis=0), preferred_element_type=jnp.float32
+    )
+    z_re, z_im = z[:LANES], z[LANES:]
+    c, s = twist[0], twist[1]
+    y = jnp.concatenate([z_re * c - z_im * s, z_re * s + z_im * c], axis=1)
+    top, rest = halves(y)
+    return over_lanes(across[...], jnp.concatenate([top, rest, top], axis=1))
 
 
 def kernel(chan, hour, norm, x, taps, bin_ids, owners, *refs):
-    tables, out = refs[:6], refs[6]
-    held = refs[7:13]
-    pick, high, low, turns, mix, back = held
-    xin, tin, ids, ids_in, xd, td, fx, fh, spec, cross, part, first, sums, second = refs[13:27]
-    table_sem, own_sem, ids_send, ids_recv, t_send, t_recv, x_send, x_recv = refs[27:35]
-    f_send, f_recv, send, recv, send2, recv2 = refs[35:]
+    tables, out = refs[:7], refs[7]
+    held = refs[8:15]
+    pick, high, low, turns, column, twist = held[:6]
+    across = held[6]
+    xin, tin, ids, ids_in, xd, td, fx, fh, spec, kron, part, first, early, outbox, inbox = refs[15:30]
+    table_sem, own_sem, ids_send, ids_recv, t_send, t_recv, x_send, x_recv = refs[30:38]
+    f_send, f_recv, send, recv, send2, recv2 = refs[38:]
     me, my_hour = lax.axis_index("chan"), lax.axis_index("hour")
     per = xin.shape[1]
     span = SPLIT * LANES
     share = pl.ds(pl.multiple_of(my_hour * (tin.shape[2] // hour), LANES), tin.shape[2] // hour)
 
-    def partner(o):
-        to, bit = me, 1
-        while bit < chan:
-            to = to + lax.rem(lax.div(o, bit), 2) * bit * (1 - 2 * lax.rem(lax.div(me, bit), 2))
+    def flipped(at, o, size):
+        to, bit = at, 1
+        while bit < size:
+            to = to + lax.rem(lax.div(o, bit), 2) * bit * (1 - 2 * lax.rem(lax.div(at, bit), 2))
             bit *= 2
         return to
+
+    def partner(o):
+        return flipped(me, o, chan)
+
+    def beside(o):
+        return flipped(my_hour, o, hour)
 
     def sent(src, dst, sends, recvs, **device):
         return pltpu.make_async_remote_copy(
@@ -290,7 +317,7 @@
         )
     for o in range(1, chan):
         pl.semaphore_signal(barrier, inc=1, device_id={"chan": partner(o)}, device_id_type=MESH)
-    place = lax.div(lax.broadcasted_iota(jnp.int32, ids.shape, 1), 8)
+    place = lax.broadcasted_iota(jnp.int32, ids.shape, 1)
     labels = jnp.zeros(ids.shape, jnp.int32)
     for r in range(ROUNDS):
         live = (place == me * ROUNDS + r) & (me >= r + 1)
@@ -404,97 +431,154 @@
     labels = ids[...]
     for o in range(1, chan):
         labels = labels + ids_in[o]
-    onehot = rows_of_pairs(labels, owners, chan, hour)
-    cross[...] = jnp.zeros_like(cross)
-
+    by_pair = rows_of_pairs(labels, owners)
+    nbins = chan * hour
+    pair = lax.broadcasted_iota(jnp.int32, (ids.shape[1], SLOTS), 0)
+    column_of = lax.broadcasted_iota(jnp.int32, (ids.shape[1], SLOTS), 1)
+    places = jnp.zeros(pair.shape, jnp.float32)
+    for s in range(1, chan):
+        for j in range(s):
+            near, far = jnp.maximum(partner(s), partner(j)), jnp.minimum(partner(s), partner(j))
+            held_by = jnp.where(near - far <= ROUNDS, near * ROUNDS + near - far - 1, -1)
+            hit = (column_of == slot_of(s, j, chan)) & (pair == held_by)
+            places = jnp.where(hit, 1.0, places)
+    by_slot = jnp.dot(by_pair, places.astype(jnp.bfloat16), preferred_element_type=jnp.float32).astype(jnp.bfloat16)
+    deep = 2 * SPLIT
+    spread = (
+        lax.div(lax.broadcasted_iota(jnp.int32, (nbins * deep, nbins), 0), deep)
+        == lax.broadcasted_iota(jnp.int32, (nbins * deep, nbins), 1)
+    ).astype(jnp.float32).astype(jnp.bfloat16)
+    widen = (
+        lax.div(lax.broadcasted_iota(jnp.int32, (SLOTS, SLOTS * deep), 1), deep)
+        == lax.broadcasted_iota(jnp.int32, (SLOTS, SLOTS * deep), 0)
+    ).astype(jnp.float32).astype(jnp.bfloat16)
+    tall = jnp.dot(spread, by_slot, preferred_element_type=jnp.float32).astype(jnp.bfloat16)
+    both = jnp.dot(tall, widen, preferred_element_type=jnp.float32)
+    same = lax.rem(lax.broadcasted_iota(jnp.int32, both.shape, 0), deep) == lax.rem(
+        lax.broadcasted_iota(jnp.int32, both.shape, 1), deep
+    )
+    kron[...] = jnp.where(same, both, 0.0).astype(jnp.bfloat16)
+
+    def cross(t, near, far, slot):
+        res, ims = [], []
+        for k2 in range(SPLIT):
+            re = im = None
+            for c in range(per // 8):
+                at = pl.ds(pl.multiple_of(near * per + 8 * c, 8), 8)
+                of = pl.ds(pl.multiple_of(far * per + 8 * c, 8), 8)
+                nr, ni = spec[t, k2, 0, at, :], spec[t, k2, 1, at, :]
+                fr, fi = spec[t, k2, 0, of, :], spec[t, k2, 1, of, :]
+                one, two = fr * nr + fi * ni, fi * nr - fr * ni
+                re, im = (one, two) if re is None else (re + one, im + two)
+            res.append(re)
+            ims.append(im)
+        part[t, slot] = jnp.concatenate([fold(res), fold(ims)], axis=0).astype(jnp.bfloat16)
+
+    def crosses(s, begin, t):
+        @pl.loop(0, s)
+        def _(j):
+            a, b = partner(s), partner(j)
+            cross(t, jnp.maximum(a, b), jnp.minimum(a, b), begin + j)
+
+    def part_copy(z, o, begin, count):
+        where = pl.ds(begin, count)
+        return sent(part.at[beside(o), where], first.at[o, where], send.at[z, o], recv.at[z, o], hour=beside(o))
+
+    groups = [(LATE, 6), (LATE + 6, 4), (LATE + 10, 5), (LATE + 15, 6), (0, 7)]
+    order = [2, 3, 1, 0]
     take(me)
 
     @pl.loop(1, chan // 2)
-    def _(o):
-        x_copy(o).wait_recv()
-        take(partner(o))
+    def _(s):
+        x_copy(s).wait_recv()
+        take(partner(s))
+
+        @pl.loop(0, TILES)
+        def _(t):
+            crosses(s, LATE + lax.div(s * (s - 1), 2), t)
+
+    for o in order[:3]:
+        part_copy(0, o, *groups[0]).start()
 
     @pl.loop(chan // 2, chan)
-    def _(o):
-        x_copy(o).wait_recv()
-        take(partner(o))
-
-    pairs = pairs_of(chan)
-    steps = SPLIT // 2
-
-    def part_copy(t, o):
-        to = lax.rem(my_hour + o, hour)
-        where = pl.ds(t * steps, steps)
-        return sent(part.at[to, where], first.at[o, where], send.at[t, o], recv.at[t, o], hour=to)
-
-    @pl.loop(0, TILES)
-    def _(t):
-        @pl.loop(0, steps)
-        def _(kk):
-            both = []
-            for e in range(2):
-                k2 = 2 * kk + e
-                for r, i in pairs:
-                    p = i * ROUNDS + r
-                    re = im = None
-                    for c in range(per // 8):
-                        near = pl.ds(i * per + 8 * c, 8)
-                        far = pl.ds((i - r - 1) * per + 8 * c, 8)
-                        nr, ni = spec[t, k2, 0, near, :], spec[t, k2, 1, near, :]
-                        fr, fi = spec[t, k2, 0, far, :], spec[t, k2, 1, far, :]
-                        one, two = fr * nr + fi * ni, fi * nr - fr * ni
-                        re, im = (one, two) if re is None else (re + one, im + two)
-                    cross[8 * p : 8 * p + 8, :LANES] = re
-                    cross[8 * p : 8 * p + 8, LANES:] = im
-                total = cross[...]
-                top = total.astype(jnp.bfloat16)
-                rest = (total - top.astype(jnp.float32)).astype(jnp.bfloat16)
-                both.append(
-                    jnp.dot(onehot, top, preferred_element_type=jnp.float32)
-                    + jnp.dot(onehot, rest, preferred_element_type=jnp.float32)
-                )
-            for h in range(hour):
-                rows_of = slice(h * chan, (h + 1) * chan)
-                part[h, t * steps + kk] = jnp.concatenate(
-                    [both[0][rows_of], both[1][rows_of]], axis=0
-                ).astype(jnp.bfloat16)
-
+    def _(s):
+        x_copy(s).wait_recv()
+        take(partner(s))
+        last = lax.div(s, chan - 1)
+        begin = (LATE + lax.div(s * (s - 1), 2)) * (1 - last)
+
+        @pl.loop(0, TILES)
+        def _(z):
+            crosses(s, begin, beside(lax.rem(z + 1, hour)))
+
+        for z in range(1, len(groups)):
+
+            @pl.when(s == z + 3)
+            def _():
+                for o in order[:3]:
+                    part_copy(z, o, *groups[z]).start()
+
+    def mixed(begin, count, room):
+        where = slice(begin, begin + count)
+        total = part[my_hour, where].astype(jnp.float32)
         for o in range(1, hour):
-            part_copy(t, o).start()
-
-    width = 2 * LANES
-    depth = chan * TILES * SPLIT
-    for t in range(TILES):
+            total = total + first[o, where].astype(jnp.float32)
+        total = total.reshape(count * deep, LANES)
+        if room > count:
+            total = jnp.concatenate([total, jnp.zeros(((room - count) * deep, LANES), jnp.float32)], axis=0)
+        got = jnp.dot(
+            kron[:, begin * deep : (begin + room) * deep],
+            jnp.concatenate(halves(total), axis=1),
+            preferred_element_type=jnp.float32,
+        )
+        return got[:, :LANES] + got[:, LANES:]
+
+    for z in range(len(groups) - 1):
         for o in range(1, hour):
-            part_copy(t, o).wait_recv()
-    total = part[my_hour].astype(jnp.float32)
+            part_copy(z, o, *groups[z]).wait_recv()
+    early[...] = mixed(LATE, 21, SLOTS - LATE)
     for o in range(1, hour):
-        total = total + first[o].astype(jnp.float32)
-    total = total.reshape(depth, width).astype(jnp.bfloat16)
-    to_row = lax.broadcasted_iota(jnp.int32, (depth, depth), 0)
-    from_row = lax.broadcasted_iota(jnp.int32, (depth, depth), 1)
-    slots = TILES * SPLIT
-    wanted = lax.rem(to_row, slots) * chan + lax.div(to_row, slots)
-    swap = (wanted == from_row).astype(jnp.float32).astype(jnp.bfloat16)
-    sums[...] = jnp.dot(swap, total, preferred_element_type=jnp.float32).astype(jnp.bfloat16).reshape(sums.shape)
-    later = []
-    for o in far_first:
-        to = partner(o)
-        later.append(sent(sums.at[to], second.at[o], send2.at[o], recv2.at[o], chan=to))
-        later[-1].start()
-    row = sums[me].astype(jnp.float32)
-    for copy in later:
-        copy.wait_recv()
-    for o in range(1, chan):
-        row = row + second[o].astype(jnp.float32)
-    out[...] = inverse(row, mix, back, high, low, norm)
-    for copy in tap_copies + id_copies + forwards + later:
+        part_copy(4, o, *groups[4]).wait_recv()
+    outbox[...] = (mixed(0, 7, LATE) + early[...]).astype(jnp.bfloat16).reshape(outbox.shape)
+    for oc in far_first + [0]:
+        for o in order:
+            if oc or o:
+                to, at = partner(oc), beside(o)
+                sent(
+                    outbox.at[to * hour + at],
+                    inbox.at[oc * hour + my_hour],
+                    send2.at[oc, o],
+                    recv2.at[oc, o],
+                    chan=to,
+                    hour=at,
+                ).start()
+    inbox[my_hour] = outbox[me * hour + my_hour]
+    for copy in tap_copies + id_copies + forwards:
         copy.wait_send()
     for o in range(1, chan):
         x_copy(o).wait_send()
-    for t in range(TILES):
+    for z in range(len(groups)):
         for o in range(1, hour):
-            part_copy(t, o).wait_send()
+            part_copy(z, o, *groups[z]).wait_send()
+
+    def out_copy(oc, o):
+        return sent(
+            outbox.at[0], inbox.at[oc * hour + beside(o)], send2.at[oc, o], recv2.at[oc, o],
+            chan=partner(oc), hour=beside(o),
+        )
+
+    for oc in range(chan):
+        for o in range(hour):
+            if oc or o:
+                out_copy(oc, o).wait_recv()
+    rows = inbox[0:hour].astype(jnp.float32)
+    for oc in range(1, chan):
+        rows = rows + inbox[oc * hour : (oc + 1) * hour].astype(jnp.float32)
+    out[...] = inverse(rows.reshape(TILES * deep, LANES), column, twist, across, norm)
+    for oc in range(chan):
+        for o in range(hour):
+            if oc or o:
+                out_copy(oc, o).wait_send()
 
 
 def split_body(traces, taps, bin_ids, owners):
@@ -503,16 +587,15 @@
     per = channels // chan
     norm = 1.0 / (FR * math.sqrt(FR * hour * channels))
     high, low = two_parts(sub_tables())
-    tables = [pick_table(), high, low, turn_table(), mix_table(), back_table()]
-    depth = 8 * ROUNDS * chan
-    slots = TILES * SPLIT
-    part = (hour, slots // 2, 2 * chan, 2 * LANES)
-    sums = (chan, slots, 2 * LANES)
+    tables = [pick_table(), high, low, turn_table(), column_table(), twist_table(), row_table()]
+    depth = LANES
+    part = (hour, SLOTS, 2 * SPLIT, LANES)
+    rows = (chan * hour, 2 * SPLIT, LANES)
     vmem, hbm = pl.BlockSpec(memory_space=pltpu.VMEM), pl.BlockSpec(memory_space=pl.ANY)
     sems = pltpu.SemaphoreType.DMA
     wave = pl.pallas_call(
         functools.partial(kernel, chan, hour, norm),
-        out_shape=jax.ShapeDtypeStruct((2 * SPLIT, SUB), jnp.float32),
+        out_shape=jax.ShapeDtypeStruct((OUT_ROWS, LANES), jnp.float32),
         in_specs=[hbm, hbm, vmem, vmem] + [hbm] * len(tables),
         out_specs=vmem,
         scratch_shapes=[pltpu.VMEM(table.shape, table.dtype) for table in tables]
@@ -526,18 +609,19 @@
             pltpu.VMEM((SPLIT, per, 2 * SUB), jnp.float32),
             pltpu.VMEM((SPLIT, channels, 2 * SUB), jnp.float32),
             pltpu.VMEM((TILES, SPLIT, 2, channels, LANES), jnp.float32),
-            pltpu.VMEM((depth, 2 * LANES), jnp.float32),
+            pltpu.VMEM((rows[0] * rows[1], SLOTS * rows[1]), jnp.bfloat16),
             pltpu.VMEM(part, jnp.bfloat16),
             pltpu.VMEM(part, jnp.bfloat16),
-            pltpu.VMEM(sums, jnp.bfloat16),
-            pltpu.VMEM(sums, jnp.bfloat16),
+            pltpu.VMEM((rows[0] * rows[1], LANES), jnp.float32),
+            pltpu.VMEM(rows, jnp.bfloat16),
+            pltpu.VMEM(rows, jnp.bfloat16),
             sems((len(tables),)),
             sems((2,)),
         ]
         + [sems((chan,))] * 6
         + [sems((hour,))] * 2
-        + [sems((TILES, hour))] * 2
-        + [sems((chan,))] * 2,
+        + [sems((5, hour))] * 2
+        + [sems((chan, hour))] * 2,
         compiler_params=pltpu.CompilerParams(
             collective_id=0, has_side_effects=True, vmem_limit_bytes=56 * 2**20
         ),
@@ -548,7 +632,7 @@
         owners.reshape(1, -1),
         *[jnp.asarray(table) for table in tables],
     )
-    return wave.reshape(2, SPLIT, SUB).transpose(0, 2, 1).reshape(1, 2 * FR)
+    return wave.reshape(1, 2 * FR)
 
 
 def solution(mesh):
@@ -559,6 +643,7 @@
         channels = traces.shape[0] // chan
         fits = (
             chan == 8
+            and hour == TILES
             and channels % (16 * chan) == 0
             and traces.shape[1] == hour * FR
             and taps.shape[1] == SPLIT * LANES // 2

time: 51.8 us -> 48.9 us (0.944)
  Pallas kernels: 49.7 us -> 47.3 us
    pallas_call x1, Pallas kernels: 49.7 us -> 47.3 us  [split_body(): pl.pallas_call(functools.partial(kernel, chan, hour, norm), out_shape=jax...]
    reshape x2 -> x0, local copies, waits for them, and re-layouts: 1.86 us -> none  [split_body(): return wave.reshape(2, SPLIT, SUB).transpose(0, 2, 1).reshape(1, 2 * FR)]
    unnamed x0 -> x1, local copies, waits for them, and re-layouts: none -> 1.38 us
where the time goes in v1:
time: 48.9 us; the launch traced here: 48.7 us
  Pallas kernels  47.3 us (97%)
  local copies, waits for them, and re-layouts  1.38 us (3%)
    pallas_call x1, Pallas kernels, split_body(): pl.pallas_call(functools.partial(kernel, chan, hour, norm), out_shape=jax...  47.3 us
    unnamed x1, local copies, waits for them, and re-layouts  1.38 us

profile of v1, /device:TPU:0, one launch (start us, length us, event | category | flops | bytes accessed | tf_op | source)
XLA Modules:
  0.0 48.7 jit_solution(3151279796245801889)
XLA Ops:
  0.0 47.3 %shard_map.109 = f32[64,128]{1,0:T(8,128)} custom-call(bf16[8,16,4096]{2,1,0:T(8,128)(2,1)} %bitcast.5, bf16[8,16,512]{2,1,0:T(8,128)(2,1)} %bitcast.7, s32[1,4]{1,0:T(1,128)} %bitcast.8, s32[1,32]{1,0:T(1,128)} %bitcast.9, bf16[1024,1024]{1,0:T(8,128)(2,1)} %constant.14.clone.refs_0_, bf16[512,1024]{1,0:T(8,128)(2,1)} %constant.15.clone.refs_1_, ...), custom_call_target="tpu_custom_call" | custom-call | tf_op jit(solution)/shard_map/pallas_call | solution.py:596
  47.3 1.4 %copy.13 = f32[1,8192]{1,0:T(1,128)} copy(f32[1,8192]{1,0:T(1,128)} %bitcast.6) | data formatting | bytes 65536

commit v2 on v1

--- a/solution.py
+++ b/solution.py
@@ -133,13 +133,17 @@
     return high, low
 
 
-def pick_table():
-    span = SPLIT * LANES
-    table = np.zeros((span, span), np.float32)
+PIECE = 512
+SHARE = PIECE // SPLIT
+
+
+def pick_tables():
+    table = np.zeros((PIECE, SPLIT, 2, SHARE), np.float32)
     for n in range(SPLIT):
-        for b in range(LANES):
-            table[SPLIT * b + n, n * LANES + b] = 1.0
-    return table.astype(jnp.bfloat16)
+        for b in range(SHARE):
+            table[SPLIT * b + n, n, :, b] = 1.0
+    twice = table.reshape(PIECE, 2 * PIECE).astype(jnp.bfloat16)
+    return np.ascontiguousarray(table[:, :, 0].reshape(PIECE, PIECE)).astype(jnp.bfloat16), twice
 
 
 def turn_table():
@@ -273,16 +277,15 @@
 
 
 def kernel(chan, hour, norm, x, taps, bin_ids, owners, *refs):
-    tables, out = refs[:7], refs[7]
-    held = refs[8:15]
+    tables, out = refs[:8], refs[8]
+    held = refs[9:17]
     pick, high, low, turns, column, twist = held[:6]
-    across = held[6]
-    xin, tin, ids, ids_in, xd, td, fx, fh, spec, kron, part, first, early, outbox, inbox = refs[15:30]
-    table_sem, own_sem, ids_send, ids_recv, t_send, t_recv, x_send, x_recv = refs[30:38]
-    f_send, f_recv, send, recv, send2, recv2 = refs[38:]
+    across, twice = held[6:]
+    xin, tin, ids, ids_in, xd, td, fx, fh, spec, kron, part, first, early, outbox, inbox = refs[17:32]
+    table_sem, own_sem, ids_send, ids_recv, t_send, t_recv, x_send, x_recv = refs[32:40]
+    f_send, f_recv, send, recv, send2, recv2 = refs[40:]
     me, my_hour = lax.axis_index("chan"), lax.axis_index("hour")
     per = xin.shape[1]
-    span = SPLIT * LANES
     share = pl.ds(pl.multiple_of(my_hour * (tin.shape[2] // hour), LANES), tin.shape[2] // hour)
 
     def flipped(at, o, size):
@@ -342,17 +345,6 @@
         id_copies[-1].start()
     for o in range(1, chan):
         x_copy(o).start()
-    own[1].wait()
-    for copy in tap_copies:
-        copy.wait_recv()
-    forwards = []
-    for o in range(1, hour):
-        to = lax.rem(my_hour + o, hour)
-        forwards.append(sent(tin.at[:, :, share], tin.at[:, :, share], f_send.at[o], f_recv.at[o], hour=to))
-        forwards[-1].start()
-    for copy in loads + own[:1]:
-        copy.wait()
-
     lane0 = lax.broadcasted_iota(jnp.int32, (8, LANES), 1) == 0
 
     def spectra(block, t, edge):
@@ -392,40 +384,49 @@
                 spec[t, k2, 0, here, :] = (xr * hr - xi * hi).astype(jnp.bfloat16).astype(jnp.float32)
                 spec[t, k2, 1, here, :] = (xr * hi + xi * hr).astype(jnp.bfloat16).astype(jnp.float32)
 
-    def take(block):
-        flat = jnp.concatenate([xin[block, :, q * span : (q + 1) * span] for q in range(FR // span)], axis=0)
-        got = jnp.dot(flat, pick[...], preferred_element_type=jnp.float32).astype(jnp.bfloat16)
-        for q in range(FR // span):
+    half = lax.broadcasted_iota(jnp.int32, (per, LANES), 1) < SHARE
+
+    def transform_of(block):
+        flat = jnp.concatenate([xin[block, :, q * PIECE : (q + 1) * PIECE] for q in range(FR // PIECE)], axis=0)
+        got = jnp.dot(flat, pick[...], preferred_element_type=jnp.float32)
+        for g in range(TILES):
             for n in range(SPLIT):
-                xd[n * per : (n + 1) * per, q * LANES : (q + 1) * LANES] = got[
-                    q * per : (q + 1) * per, n * LANES : (n + 1) * LANES
-                ]
+                a, b = (
+                    got[q * per : (q + 1) * per, n // 2 * LANES : (n // 2 + 1) * LANES] for q in (2 * g, 2 * g + 1)
+                )
+                if n % 2:
+                    a = pltpu.roll(a, SHARE, 1)
+                else:
+                    b = pltpu.roll(b, SHARE, 1)
+                xd[n * per : (n + 1) * per, g * LANES : (g + 1) * LANES] = jnp.where(half, a, b).astype(jnp.bfloat16)
         found = jnp.dot(xd[...], high[...], preferred_element_type=jnp.float32) + jnp.dot(
             xd[...], low[...], preferred_element_type=jnp.float32
         )
         for n in range(SPLIT):
             fx[n] = found[n * per : (n + 1) * per]
+
+    def spectra_of(block):
         spectra(block, 0, True)
 
         @pl.loop(1, TILES)
         def _(t):
             spectra(block, t, False)
 
-    for copy in forwards:
+    def take(block):
+        transform_of(block)
+        spectra_of(block)
+
+    for copy in loads + own[:1]:
+        copy.wait()
+    transform_of(me)
+    own[1].wait()
+    for copy in tap_copies:
         copy.wait_recv()
-    count = tin.shape[2]
-    got = jnp.dot(
-        tin[...].reshape(chan * per, count), pick[:count, :], preferred_element_type=jnp.float32
-    ).astype(jnp.bfloat16)
-    for n in range(SPLIT):
-        td[n] = got[:, n * LANES : (n + 1) * LANES]
-
-    @pl.loop(0, SPLIT)
-    def _(n):
-        fh[n] = jnp.dot(td[n], high[:LANES, :], preferred_element_type=jnp.float32) + jnp.dot(
-            td[n], low[:LANES, :], preferred_element_type=jnp.float32
-        )
-
+    forwards = []
+    for o in range(1, hour):
+        to = lax.rem(my_hour + o, hour)
+        forwards.append(sent(tin.at[:, :, share], tin.at[:, :, share], f_send.at[o], f_recv.at[o], hour=to))
+        forwards[-1].start()
     for copy in id_copies:
         copy.wait_recv()
     labels = ids[...]
@@ -474,11 +475,12 @@
             ims.append(im)
         part[t, slot] = jnp.concatenate([fold(res), fold(ims)], axis=0).astype(jnp.bfloat16)
 
-    def crosses(s, begin, t):
+    def crosses(s, begin):
         @pl.loop(0, s)
         def _(j):
             a, b = partner(s), partner(j)
-            cross(t, jnp.maximum(a, b), jnp.minimum(a, b), begin + j)
+            for t in range(TILES):
+                cross(t, jnp.maximum(a, b), jnp.minimum(a, b), begin + j)
 
     def part_copy(z, o, begin, count):
         where = pl.ds(begin, count)
@@ -486,16 +488,26 @@
 
     groups = [(LATE, 6), (LATE + 6, 4), (LATE + 10, 5), (LATE + 15, 6), (0, 7)]
     order = [2, 3, 1, 0]
-    take(me)
+    for copy in forwards:
+        copy.wait_recv()
+    count = tin.shape[2]
+    got = jnp.dot(tin[...].reshape(chan * per, count), twice[...], preferred_element_type=jnp.float32)
+    for n in range(SPLIT):
+        td[n] = got[:, n * LANES : (n + 1) * LANES].astype(jnp.bfloat16)
+    found = jnp.dot(
+        td[...].reshape(SPLIT * chan * per, LANES),
+        jnp.concatenate([high[:SHARE, :], low[:SHARE, :]], axis=0),
+        preferred_element_type=jnp.float32,
+    )
+    for n in range(SPLIT):
+        fh[n] = found[n * chan * per : (n + 1) * chan * per]
+    spectra_of(me)
 
     @pl.loop(1, chan // 2)
     def _(s):
         x_copy(s).wait_recv()
         take(partner(s))
-
-        @pl.loop(0, TILES)
-        def _(t):
-            crosses(s, LATE + lax.div(s * (s - 1), 2), t)
+        crosses(s, LATE + lax.div(s * (s - 1), 2))
 
     for o in order[:3]:
         part_copy(0, o, *groups[0]).start()
@@ -507,9 +519,7 @@
         last = lax.div(s, chan - 1)
         begin = (LATE + lax.div(s * (s - 1), 2)) * (1 - last)
 
-        @pl.loop(0, TILES)
-        def _(z):
-            crosses(s, begin, beside(lax.rem(z + 1, hour)))
+        crosses(s, begin)
 
         for z in range(1, len(groups)):
 
@@ -574,7 +584,9 @@
     rows = inbox[0:hour].astype(jnp.float32)
     for oc in range(1, chan):
         rows = rows + inbox[oc * hour : (oc + 1) * hour].astype(jnp.float32)
-    out[...] = inverse(rows.reshape(TILES * deep, LANES), column, twist, across, norm)
+    wave = inverse(rows.reshape(TILES * deep, LANES), column, twist, across, norm)
+    for u in range(OUT_ROWS):
+        out[:, u * LANES : (u + 1) * LANES] = wave[u : u + 1]
     for oc in range(chan):
         for o in range(hour):
             if oc or o:
@@ -587,7 +599,8 @@
     per = channels // chan
     norm = 1.0 / (FR * math.sqrt(FR * hour * channels))
     high, low = two_parts(sub_tables())
-    tables = [pick_table(), high, low, turn_table(), column_table(), twist_table(), row_table()]
+    pick, twice = pick_tables()
+    tables = [pick, high, low, turn_table(), column_table(), twist_table(), row_table(), twice]
     depth = LANES
     part = (hour, SLOTS, 2 * SPLIT, LANES)
     rows = (chan * hour, 2 * SPLIT, LANES)
@@ -595,7 +608,7 @@
     sems = pltpu.SemaphoreType.DMA
     wave = pl.pallas_call(
         functools.partial(kernel, chan, hour, norm),
-        out_shape=jax.ShapeDtypeStruct((OUT_ROWS, LANES), jnp.float32),
+        out_shape=jax.ShapeDtypeStruct((1, 2 * FR), jnp.float32),
         in_specs=[hbm, hbm, vmem, vmem] + [hbm] * len(tables),
         out_specs=vmem,
         scratch_shapes=[pltpu.VMEM(table.shape, table.dtype) for table in tables]
@@ -632,7 +645,7 @@
         owners.reshape(1, -1),
         *[jnp.asarray(table) for table in tables],
     )
-    return wave.reshape(1, 2 * FR)
+    return wave
 
 
 def solution(mesh):

time: 48.9 us -> 47.1 us (0.963)
  Pallas kernels: 47.3 us -> 45.6 us
    pallas_call x1, Pallas kernels: 47.3 us -> 45.6 us  [split_body(): pl.pallas_call(functools.partial(kernel, chan, hour, norm), out_shape=jax...]
where the time goes in v2:
time: 47.1 us; the launch traced here: 46.9 us
  Pallas kernels  45.6 us (97%)
  local copies, waits for them, and re-layouts  1.38 us (3%)
    pallas_call x1, Pallas kernels, split_body(): pl.pallas_call(functools.partial(kernel, chan, hour, norm), out_shape=jax...  45.6 us
    unnamed x1, local copies, waits for them, and re-layouts  1.38 us

profile of v2, /device:TPU:0, one launch (start us, length us, event | category | flops | bytes accessed | tf_op | source)
XLA Modules:
  0.0 46.9 jit_solution(17689212024989615755)
XLA Ops:
  0.0 45.6 %shard_map.118 = f32[1,8192]{1,0:T(1,128)} custom-call(bf16[8,16,4096]{2,1,0:T(8,128)(2,1)} %bitcast.4, bf16[8,16,512]{2,1,0:T(8,128)(2,1)} %bitcast.5, s32[1,4]{1,0:T(1,128)} %bitcast.6, s32[1,32]{1,0:T(1,128)} %bitcast.7, bf16[512,512]{1,0:T(8,128)(2,1)} %constant.16.clone.refs_0_, bf16[512,1024]{1,0:T(8,128)(2,1)} %constant.17.clone.refs_1_, ...), custom_call_target="tpu_custom_call" | custom-call | tf_op jit(solution)/shard_map/pallas_call | solution.py:609
  45.6 1.4 %copy.14 = f32[1,8192]{1,0:T(1,128)} copy(f32[1,8192]{1,0:T(1,128)} %shard_map.118) | data formatting | bytes 65536

commit v3 on v2

--- a/solution.py
+++ b/solution.py
@@ -256,10 +256,10 @@
     return lax.dot_general(a, b, (((1,), (1,)), ((), ())), preferred_element_type=jnp.float32)
 
 
-def inverse(rows, column, twist, across, norm):
+def inverse(rows, column, twist, across):
     lane = lax.broadcasted_iota(jnp.int32, rows.shape, 1)
     slot = lax.broadcasted_iota(jnp.int32, rows.shape, 0)
-    rows = rows * jnp.where((lane == 0) & (slot == 0), norm, 2.0 * norm)
+    rows = rows * jnp.where((lane == 0) & (slot == 0), 1.0, 2.0)
     apart = (lane == 0) & (slot < 2 * SPLIT) & (lax.rem(slot, SPLIT) >= SPLIT // 2)
     every = jnp.concatenate(
         [jnp.where(apart, 0.0, rows), jnp.where(apart, rows, 0.0)[: 2 * SPLIT]], axis=0
@@ -276,7 +276,7 @@
     return over_lanes(across[...], jnp.concatenate([top, rest, top], axis=1))
 
 
-def kernel(chan, hour, norm, x, taps, bin_ids, owners, *refs):
+def kernel(chan, hour, x, taps, bin_ids, owners, *refs):
     tables, out = refs[:8], refs[8]
     held = refs[9:17]
     pick, high, low, turns, column, twist = held[:6]
@@ -512,21 +512,43 @@
     for o in order[:3]:
         part_copy(0, o, *groups[0]).start()
 
-    @pl.loop(chan // 2, chan)
+    @pl.loop(chan // 2, chan - 1)
     def _(s):
         x_copy(s).wait_recv()
         take(partner(s))
-        last = lax.div(s, chan - 1)
-        begin = (LATE + lax.div(s * (s - 1), 2)) * (1 - last)
-
-        crosses(s, begin)
-
-        for z in range(1, len(groups)):
+        crosses(s, LATE + lax.div(s * (s - 1), 2))
+
+        for z in range(1, len(groups) - 1):
 
             @pl.when(s == z + 3)
             def _():
                 for o in order[:3]:
                     part_copy(z, o, *groups[z]).start()
+
+    x_copy(chan - 1).wait_recv()
+    block = partner(chan - 1)
+    transform_of(block)
+
+    @pl.loop(0, TILES)
+    def _(z):
+        late = lax.div(z, 2)
+        o = (1 - late) * (2 + z) + late * (3 - z)
+        t = beside(o)
+
+        @pl.when(t == 0)
+        def _():
+            spectra(block, 0, True)
+
+        @pl.when(t > 0)
+        def _():
+            spectra(block, t, False)
+
+        for j in range(chan - 1):
+            cross(t, jnp.maximum(block, partner(j)), jnp.minimum(block, partner(j)), j)
+
+        @pl.when(o > 0)
+        def _():
+            part_copy(4, o, *groups[4]).start()
 
     def mixed(begin, count, room):
         where = slice(begin, begin + count)
@@ -557,8 +579,8 @@
                 sent(
                     outbox.at[to * hour + at],
                     inbox.at[oc * hour + my_hour],
-                    send2.at[oc, o],
-                    recv2.at[oc, o],
+                    send2.at[0],
+                    recv2.at[0],
                     chan=to,
                     hour=at,
                 ).start()
@@ -571,26 +593,16 @@
         for o in range(1, hour):
             part_copy(z, o, *groups[z]).wait_send()
 
-    def out_copy(oc, o):
-        return sent(
-            outbox.at[0], inbox.at[oc * hour + beside(o)], send2.at[oc, o], recv2.at[oc, o],
-            chan=partner(oc), hour=beside(o),
-        )
-
-    for oc in range(chan):
-        for o in range(hour):
-            if oc or o:
-                out_copy(oc, o).wait_recv()
+    others = pl.ds(0, chan * hour - 1)
+    all_rows = sent(outbox.at[others], inbox.at[others], send2.at[0], recv2.at[0], chan=partner(1))
+    all_rows.wait_recv()
     rows = inbox[0:hour].astype(jnp.float32)
     for oc in range(1, chan):
         rows = rows + inbox[oc * hour : (oc + 1) * hour].astype(jnp.float32)
-    wave = inverse(rows.reshape(TILES * deep, LANES), column, twist, across, norm)
+    wave = inverse(rows.reshape(TILES * deep, LANES), column, twist, across)
     for u in range(OUT_ROWS):
         out[:, u * LANES : (u + 1) * LANES] = wave[u : u + 1]
-    for oc in range(chan):
-        for o in range(hour):
-            if oc or o:
-                out_copy(oc, o).wait_send()
+    all_rows.wait_send()
 
 
 def split_body(traces, taps, bin_ids, owners):
@@ -607,7 +619,7 @@
     vmem, hbm = pl.BlockSpec(memory_space=pltpu.VMEM), pl.BlockSpec(memory_space=pl.ANY)
     sems = pltpu.SemaphoreType.DMA
     wave = pl.pallas_call(
-        functools.partial(kernel, chan, hour, norm),
+        functools.partial(kernel, chan, hour),
         out_shape=jax.ShapeDtypeStruct((1, 2 * FR), jnp.float32),
         in_specs=[hbm, hbm, vmem, vmem] + [hbm] * len(tables),
         out_specs=vmem,
@@ -634,7 +646,7 @@
         + [sems((chan,))] * 6
         + [sems((hour,))] * 2
         + [sems((5, hour))] * 2
-        + [sems((chan, hour))] * 2,
+        + [sems((1,))] * 2,
         compiler_params=pltpu.CompilerParams(
             collective_id=0, has_side_effects=True, vmem_limit_bytes=56 * 2**20
         ),
@@ -645,7 +657,7 @@
         owners.reshape(1, -1),
         *[jnp.asarray(table) for table in tables],
     )
-    return wave
+    return wave * norm
 
 
 def solution(mesh):

time: 47.1 us -> 45.5 us (0.966)
  Pallas kernels: 45.6 us -> 43.9 us
  other arithmetic: 0 us -> 1.41 us
  local copies, waits for them, and re-layouts: 1.38 us -> 0 us
    pallas_call x1, Pallas kernels: 45.6 us -> 43.9 us  [split_body(): pl.pallas_call(functools.partial(kernel, chan, hour), out_shape=jax.Shape...]
    mul x0 -> x1, other arithmetic: none -> 1.41 us  [split_body(): return wave * norm]
    unnamed x1 -> x0, local copies, waits for them, and re-layouts: 1.38 us -> none
where the time goes in v3:
time: 45.5 us; the launch traced here: 45.3 us
  Pallas kernels  43.9 us (96%)
  other arithmetic  1.41 us (3%)
    pallas_call x1, Pallas kernels, split_body(): pl.pallas_call(functools.partial(kernel, chan, hour), out_shape=jax.Shape...  43.9 us
    mul x1, other arithmetic, split_body(): return wave * norm  1.41 us

profile of v3, /device:TPU:0, one launch (start us, length us, event | category | flops | bytes accessed | tf_op | source)
XLA Modules:
  0.0 45.3 jit_solution(14769125742019073543)
XLA Ops:
  0.0 43.9 %shard_map.118 = f32[1,8192]{1,0:T(1,128)} custom-call(bf16[8,16,4096]{2,1,0:T(8,128)(2,1)} %bitcast.4, bf16[8,16,512]{2,1,0:T(8,128)(2,1)} %bitcast.5, s32[1,4]{1,0:T(1,128)} %bitcast.6, s32[1,32]{1,0:T(1,128)} %bitcast.7, bf16[512,512]{1,0:T(8,128)(2,1)} %constant.18.clone.refs_0_, bf16[512,1024]{1,0:T(8,128)(2,1)} %constant.19.clone.refs_1_, ...), custom_call_target="tpu_custom_call" | custom-call | tf_op jit(solution)/shard_map/pallas_call | solution.py:621
  43.9 1.4 %broadcast_multiply_fusion = f32[1,8192]{1,0:T(1,128)} fusion(f32[1,8192]{1,0:T(1,128)} %shard_map.118), kind=kLoop, calls=%fused_computation | loop fusion | flops 8192 | bytes 65536 | tf_op jit(solution)/shard_map/mul | solution.py:660

commit v4 on v3

--- a/solution.py
+++ b/solution.py
@@ -311,8 +311,6 @@
         pltpu.make_async_copy(x.at[me], xin.at[me], own_sem.at[0]),
         pltpu.make_async_copy(taps.at[me, :, share], tin.at[me, :, share], own_sem.at[1]),
     ]
-    for copy in own + loads:
-        copy.start()
     barrier = pltpu.get_barrier_semaphore()
     for o in range(1, hour):
         pl.semaphore_signal(
@@ -320,6 +318,8 @@
         )
     for o in range(1, chan):
         pl.semaphore_signal(barrier, inc=1, device_id={"chan": partner(o)}, device_id_type=MESH)
+    for copy in own + loads:
+        copy.start()
     place = lax.broadcasted_iota(jnp.int32, ids.shape, 1)
     labels = jnp.zeros(ids.shape, jnp.int32)
     for r in range(ROUNDS):
@@ -341,7 +341,9 @@
         )
         tap_copies[-1].start()
     for o in far_first:
-        id_copies.append(sent(ids, ids_in.at[o], ids_send.at[o], ids_recv.at[o], chan=partner(o)))
+        id_copies.append(
+            sent(ids.at[0:1], ids_in.at[o, 0:1], ids_send.at[o], ids_recv.at[o], chan=partner(o))
+        )
         id_copies[-1].start()
     for o in range(1, chan):
         x_copy(o).start()
@@ -429,9 +431,9 @@
         forwards[-1].start()
     for copy in id_copies:
         copy.wait_recv()
-    labels = ids[...]
+    labels = ids[0:1, :]
     for o in range(1, chan):
-        labels = labels + ids_in[o]
+        labels = labels + ids_in[o, 0:1, :]
     by_pair = rows_of_pairs(labels, owners)
     nbins = chan * hour
     pair = lax.broadcasted_iota(jnp.int32, (ids.shape[1], SLOTS), 0)
@@ -600,8 +602,7 @@
     for oc in range(1, chan):
         rows = rows + inbox[oc * hour : (oc + 1) * hour].astype(jnp.float32)
     wave = inverse(rows.reshape(TILES * deep, LANES), column, twist, across)
-    for u in range(OUT_ROWS):
-        out[:, u * LANES : (u + 1) * LANES] = wave[u : u + 1]
+    out[...] = wave
     all_rows.wait_send()
 
 
@@ -620,7 +621,7 @@
     sems = pltpu.SemaphoreType.DMA
     wave = pl.pallas_call(
         functools.partial(kernel, chan, hour),
-        out_shape=jax.ShapeDtypeStruct((1, 2 * FR), jnp.float32),
+        out_shape=pltpu.VMEM((OUT_ROWS, LANES), jnp.float32),
         in_specs=[hbm, hbm, vmem, vmem] + [hbm] * len(tables),
         out_specs=vmem,
         scratch_shapes=[pltpu.VMEM(table.shape, table.dtype) for table in tables]
@@ -657,7 +658,7 @@
         owners.reshape(1, -1),
         *[jnp.asarray(table) for table in tables],
     )
-    return wave * norm
+    return (wave * norm).reshape(1, 2 * FR)
 
 
 def solution(mesh):

time: 45.5 us -> 43.4 us (0.954)
  Pallas kernels: 43.9 us -> 42.6 us
  other arithmetic: 1.41 us -> 0.62 us
    pallas_call x1, Pallas kernels: 43.9 us -> 42.6 us  [split_body(): pl.pallas_call(functools.partial(kernel, chan, hour), out_shape=pltpu.VME...]
    mul x1, other arithmetic: 1.41 us -> 0.62 us  [split_body(): return (wave * norm).reshape(1, 2 * FR)]
where the time goes in v4:
time: 43.4 us; the launch traced here: 43.3 us
  Pallas kernels  42.6 us (98%)
  other arithmetic  0.62 us (1%)
    pallas_call x1, Pallas kernels, split_body(): pl.pallas_call(functools.partial(kernel, chan, hour), out_shape=pltpu.VME...  42.6 us

profile of v4, /device:TPU:0, one launch (start us, length us, event | category | flops | bytes accessed | tf_op | source)
XLA Modules:
  0.0 43.3 jit_solution(14435233860445514058)
XLA Ops:
  0.0 42.6 %shard_map.118 = f32[64,128]{1,0:T(8,128)S(1)} custom-call(bf16[8,16,4096]{2,1,0:T(8,128)(2,1)} %bitcast.5, bf16[8,16,512]{2,1,0:T(8,128)(2,1)} %bitcast.6, s32[1,4]{1,0:T(1,128)} %bitcast.7, s32[1,32]{1,0:T(1,128)} %bitcast.8, bf16[512,512]{1,0:T(8,128)(2,1)} %constant.18.clone.refs_0_, bf16[512,1024]{1,0:T(8,128)(2,1)} %constant.19.clone.refs_1_, ...), custom_call_target="tpu_custom_call" | custom-call | tf_op jit(solution)/shard_map/pallas_call | solution.py:622
  42.7 0.6 %broadcast_multiply_fusion = f32[64,128]{1,0:T(8,128)} fusion(f32[64,128]{1,0:T(8,128)S(1)} %shard_map.118), kind=kLoop, calls=%fused_computation | loop fusion | flops 8192 | bytes 65536 | tf_op jit(solution)/shard_map/mul | solution.py:661

commit v5 on v4

--- a/solution.py
+++ b/solution.py
@@ -277,13 +277,13 @@
 
 
 def kernel(chan, hour, x, taps, bin_ids, owners, *refs):
-    tables, out = refs[:8], refs[8]
-    held = refs[9:17]
-    pick, high, low, turns, column, twist = held[:6]
-    across, twice = held[6:]
-    xin, tin, ids, ids_in, xd, td, fx, fh, spec, kron, part, first, early, outbox, inbox = refs[17:32]
-    table_sem, own_sem, ids_send, ids_recv, t_send, t_recv, x_send, x_recv = refs[32:40]
-    f_send, f_recv, send, recv, send2, recv2 = refs[40:]
+    tables, out = refs[:7], refs[7]
+    held = refs[8:15]
+    pick, high, turns, column, twist = held[:5]
+    across, twice = held[5:]
+    xin, tin, ids, ids_in, xd, td, fx, fh, spec, kron, part, first, early, outbox, inbox = refs[15:30]
+    table_sem, own_sem, ids_send, ids_recv, t_send, t_recv, x_send, x_recv = refs[30:38]
+    f_send, f_recv, send, recv, send2, recv2 = refs[38:]
     me, my_hour = lax.axis_index("chan"), lax.axis_index("hour")
     per = xin.shape[1]
     share = pl.ds(pl.multiple_of(my_hour * (tin.shape[2] // hour), LANES), tin.shape[2] // hour)
@@ -349,40 +349,41 @@
         x_copy(o).start()
     lane0 = lax.broadcasted_iota(jnp.int32, (8, LANES), 1) == 0
 
+    def bins_of(f, rows, t, edge):
+        values, extra = [], []
+        for n in range(SPLIT):
+            re = f[n, rows, pl.ds(pl.multiple_of(2 * t * LANES, LANES), LANES)]
+            im = f[n, rows, pl.ds(pl.multiple_of((2 * t + 1) * LANES, LANES), LANES)]
+            if edge:
+                angle = -math.pi * n / SPLIT
+                extra.append((im * math.cos(angle), im * math.sin(angle)))
+                im = jnp.where(lane0, 0.0, im)
+            if n == 0:
+                values.append((re, im))
+            else:
+                c, s = turns[t, n, 0], turns[t, n, 1]
+                values.append((re * c - im * s, re * s + im * c))
+        found = small_dft(values, -1)
+        if edge:
+            more = small_dft(extra, -1, half=True)
+            for k2 in range(SPLIT // 2):
+                old = found[SPLIT // 2 + k2]
+                found[SPLIT // 2 + k2] = tuple(jnp.where(lane0, more[k2][z], old[z]) for z in range(2))
+        return found
+
+    def responses(t, edge):
+        @pl.loop(0, chan * per // 8)
+        def _(g):
+            here = pl.ds(pl.multiple_of(8 * g, 8), 8)
+            for k2, (hr, hi) in enumerate(bins_of(fh, here, t, edge)):
+                spec[t, k2, 0, here, :] = hr
+                spec[t, k2, 1, here, :] = hi
+
     def spectra(block, t, edge):
-        @pl.loop(0, per // 8)
-        def _(g):
-            piece = pl.ds(pl.multiple_of(8 * g, 8), 8)
+        for g in range(per // 8):
             here = pl.ds(pl.multiple_of(block * per + 8 * g, 8), 8)
-
-            def bins_of(f, rows):
-                values, extra = [], []
-                for n in range(SPLIT):
-                    re = f[n, rows, pl.ds(pl.multiple_of(2 * t * LANES, LANES), LANES)]
-                    im = f[n, rows, pl.ds(pl.multiple_of((2 * t + 1) * LANES, LANES), LANES)]
-                    if edge:
-                        angle = -math.pi * n / SPLIT
-                        extra.append((im * math.cos(angle), im * math.sin(angle)))
-                        im = jnp.where(lane0, 0.0, im)
-                    if n == 0:
-                        values.append((re, im))
-                    else:
-                        c, s = turns[t, n, 0], turns[t, n, 1]
-                        values.append((re * c - im * s, re * s + im * c))
-                found = small_dft(values, -1)
-                if edge:
-                    more = small_dft(extra, -1, half=True)
-                    for k2 in range(SPLIT // 2):
-                        old = found[SPLIT // 2 + k2]
-                        found[SPLIT // 2 + k2] = tuple(
-                            jnp.where(lane0, more[k2][z], old[z]) for z in range(2)
-                        )
-                return found
-
-            freq = bins_of(fx, piece)
-            resp = bins_of(fh, here)
-            for k2 in range(SPLIT):
-                (xr, xi), (hr, hi) = freq[k2], resp[k2]
+            for k2, (xr, xi) in enumerate(bins_of(fx, slice(8 * g, 8 * g + 8), t, edge)):
+                hr, hi = spec[t, k2, 0, here, :], spec[t, k2, 1, here, :]
                 spec[t, k2, 0, here, :] = (xr * hr - xi * hi).astype(jnp.bfloat16).astype(jnp.float32)
                 spec[t, k2, 1, here, :] = (xr * hi + xi * hr).astype(jnp.bfloat16).astype(jnp.float32)
 
@@ -401,9 +402,7 @@
                 else:
                     b = pltpu.roll(b, SHARE, 1)
                 xd[n * per : (n + 1) * per, g * LANES : (g + 1) * LANES] = jnp.where(half, a, b).astype(jnp.bfloat16)
-        found = jnp.dot(xd[...], high[...], preferred_element_type=jnp.float32) + jnp.dot(
-            xd[...], low[...], preferred_element_type=jnp.float32
-        )
+        found = jnp.dot(jnp.concatenate([xd[...], xd[...]], axis=1), high[...], preferred_element_type=jnp.float32)
         for n in range(SPLIT):
             fx[n] = found[n * per : (n + 1) * per]
 
@@ -498,11 +497,17 @@
         td[n] = got[:, n * LANES : (n + 1) * LANES].astype(jnp.bfloat16)
     found = jnp.dot(
         td[...].reshape(SPLIT * chan * per, LANES),
-        jnp.concatenate([high[:SHARE, :], low[:SHARE, :]], axis=0),
+        jnp.concatenate([high[:SHARE, :], high[SUB : SUB + SHARE, :]], axis=0),
         preferred_element_type=jnp.float32,
     )
     for n in range(SPLIT):
         fh[n] = found[n * chan * per : (n + 1) * chan * per]
+    responses(0, True)
+
+    @pl.loop(1, TILES)
+    def _(t):
+        responses(t, False)
+
     spectra_of(me)
 
     @pl.loop(1, chan // 2)
@@ -613,7 +618,7 @@
     norm = 1.0 / (FR * math.sqrt(FR * hour * channels))
     high, low = two_parts(sub_tables())
     pick, twice = pick_tables()
-    tables = [pick, high, low, turn_table(), column_table(), twist_table(), row_table(), twice]
+    tables = [pick, np.concatenate([high, low], axis=0), turn_table(), column_table(), twist_table(), row_table(), twice]
     depth = LANES
     part = (hour, SLOTS, 2 * SPLIT, LANES)
     rows = (chan * hour, 2 * SPLIT, LANES)

time: 43.4 us -> 42.9 us (0.988)
  Pallas kernels: 42.6 us -> 42.1 us
    pallas_call x1, Pallas kernels: 42.6 us -> 42.1 us  [split_body(): pl.pallas_call(functools.partial(kernel, chan, hour), out_shape=pltpu.VME...]
where the time goes in v5:
time: 42.9 us; the launch traced here: 42.7 us
  Pallas kernels  42.1 us (98%)
  other arithmetic  0.62 us (1%)
    pallas_call x1, Pallas kernels, split_body(): pl.pallas_call(functools.partial(kernel, chan, hour), out_shape=pltpu.VME...  42.1 us

profile of v5, /device:TPU:0, one launch (start us, length us, event | category | flops | bytes accessed | tf_op | source)
XLA Modules:
  0.0 42.7 jit_solution(3196992954238109465)
XLA Ops:
  0.0 42.1 %shard_map.109 = f32[64,128]{1,0:T(8,128)S(1)} custom-call(bf16[8,16,4096]{2,1,0:T(8,128)(2,1)} %bitcast.5, bf16[8,16,512]{2,1,0:T(8,128)(2,1)} %bitcast.6, s32[1,4]{1,0:T(1,128)} %bitcast.7, s32[1,32]{1,0:T(1,128)} %bitcast.8, bf16[512,512]{1,0:T(8,128)(2,1)} %constant.16.clone.refs_0_, bf16[1024,1024]{1,0:T(8,128)(2,1)} %constant.17.clone.refs_1_, ...), custom_call_target="tpu_custom_call" | custom-call | tf_op jit(solution)/shard_map/pallas_call | solution.py:627
  42.1 0.6 %broadcast_multiply_fusion = f32[64,128]{1,0:T(8,128)} fusion(f32[64,128]{1,0:T(8,128)S(1)} %shard_map.109), kind=kLoop, calls=%fused_computation | loop fusion | flops 8192 | bytes 65536 | tf_op jit(solution)/shard_map/mul | solution.py:666

commit v6 on v5

--- a/solution.py
+++ b/solution.py
@@ -557,7 +557,7 @@
         def _():
             part_copy(4, o, *groups[4]).start()
 
-    def mixed(begin, count, room):
+    def summed(begin, count, room):
         where = slice(begin, begin + count)
         total = part[my_hour, where].astype(jnp.float32)
         for o in range(1, hour):
@@ -565,32 +565,40 @@
         total = total.reshape(count * deep, LANES)
         if room > count:
             total = jnp.concatenate([total, jnp.zeros(((room - count) * deep, LANES), jnp.float32)], axis=0)
+        return jnp.concatenate(halves(total), axis=1)
+
+    def mixed(rows, begin, room, values):
         got = jnp.dot(
-            kron[:, begin * deep : (begin + room) * deep],
-            jnp.concatenate(halves(total), axis=1),
-            preferred_element_type=jnp.float32,
+            kron[rows, begin * deep : (begin + room) * deep], values, preferred_element_type=jnp.float32
         )
         return got[:, :LANES] + got[:, LANES:]
 
     for z in range(len(groups) - 1):
         for o in range(1, hour):
             part_copy(z, o, *groups[z]).wait_recv()
-    early[...] = mixed(LATE, 21, SLOTS - LATE)
+    early[...] = mixed(slice(None), LATE, SLOTS - LATE, summed(LATE, 21, SLOTS - LATE))
     for o in range(1, hour):
         part_copy(4, o, *groups[4]).wait_recv()
-    outbox[...] = (mixed(0, 7, LATE) + early[...]).astype(jnp.bfloat16).reshape(outbox.shape)
-    for oc in far_first + [0]:
-        for o in order:
-            if oc or o:
-                to, at = partner(oc), beside(o)
-                sent(
-                    outbox.at[to * hour + at],
-                    inbox.at[oc * hour + my_hour],
-                    send2.at[0],
-                    recv2.at[0],
-                    chan=to,
-                    hour=at,
-                ).start()
+    late = summed(0, 7, LATE)
+    side = nbins // 2
+    for z in range(2):
+        half_of = 1 - lax.div(me, chan // 2) if z == 0 else lax.div(me, chan // 2)
+        deep_rows = pl.ds(pl.multiple_of(half_of * side * deep, side * deep), side * deep)
+        outbox[pl.ds(half_of * side, side)] = (
+            (mixed(deep_rows, 0, LATE, late) + early[deep_rows, :]).astype(jnp.bfloat16).reshape(side, deep, LANES)
+        )
+        for oc in (5, 4, 7, 6) if z == 0 else (3, 2, 1, 0):
+            for o in order:
+                if oc or o:
+                    to, at = partner(oc), beside(o)
+                    sent(
+                        outbox.at[to * hour + at],
+                        inbox.at[oc * hour + my_hour],
+                        send2.at[0],
+                        recv2.at[0],
+                        chan=to,
+                        hour=at,
+                    ).start()
     inbox[my_hour] = outbox[me * hour + my_hour]
     for copy in tap_copies + id_copies + forwards:
         copy.wait_send()

time: 42.9 us -> 42.5 us (level)
  no operation moved by 1% of the time
where the time goes in v6:
time: 42.5 us; the launch traced here: 42.3 us
  Pallas kernels  41.7 us (98%)
  other arithmetic  0.62 us (1%)
    pallas_call x1, Pallas kernels, split_body(): pl.pallas_call(functools.partial(kernel, chan, hour), out_shape=pltpu.VME...  41.7 us

profile of v6, /device:TPU:0, one launch (start us, length us, event | category | flops | bytes accessed | tf_op | source)
XLA Modules:
  0.0 42.3 jit_solution(12277210886338295903)
XLA Ops:
  0.0 41.7 %shard_map.109 = f32[64,128]{1,0:T(8,128)S(1)} custom-call(bf16[8,16,4096]{2,1,0:T(8,128)(2,1)} %bitcast.5, bf16[8,16,512]{2,1,0:T(8,128)(2,1)} %bitcast.6, s32[1,4]{1,0:T(1,128)} %bitcast.7, s32[1,32]{1,0:T(1,128)} %bitcast.8, bf16[512,512]{1,0:T(8,128)(2,1)} %constant.16.clone.refs_0_, bf16[1024,1024]{1,0:T(8,128)(2,1)} %constant.17.clone.refs_1_, ...), custom_call_target="tpu_custom_call" | custom-call | tf_op jit(solution)/shard_map/pallas_call | solution.py:635
  41.7 0.6 %broadcast_multiply_fusion = f32[64,128]{1,0:T(8,128)} fusion(f32[64,128]{1,0:T(8,128)S(1)} %shard_map.109), kind=kLoop, calls=%fused_computation | loop fusion | flops 8192 | bytes 65536 | tf_op jit(solution)/shard_map/mul | solution.py:674

commit v7 on v6

--- a/solution.py
+++ b/solution.py
@@ -588,7 +588,7 @@
             (mixed(deep_rows, 0, LATE, late) + early[deep_rows, :]).astype(jnp.bfloat16).reshape(side, deep, LANES)
         )
         for oc in (5, 4, 7, 6) if z == 0 else (3, 2, 1, 0):
-            for o in order:
+            for o in (0, 1, 2, 3):
                 if oc or o:
                     to, at = partner(oc), beside(o)
                     sent(

time: 42.5 us -> 42.3 us (level)
  no operation moved by 1% of the time
where the time goes in v7:
time: 42.3 us; the launch traced here: 42.1 us
  Pallas kernels  41.5 us (98%)
  other arithmetic  0.62 us (1%)
    pallas_call x1, Pallas kernels, split_body(): pl.pallas_call(functools.partial(kernel, chan, hour), out_shape=pltpu.VME...  41.5 us

profile of v7, /device:TPU:0, one launch (start us, length us, event | category | flops | bytes accessed | tf_op | source)
XLA Modules:
  0.0 42.1 jit_solution(14623131113859411222)
XLA Ops:
  0.0 41.5 %shard_map.109 = f32[64,128]{1,0:T(8,128)S(1)} custom-call(bf16[8,16,4096]{2,1,0:T(8,128)(2,1)} %bitcast.5, bf16[8,16,512]{2,1,0:T(8,128)(2,1)} %bitcast.6, s32[1,4]{1,0:T(1,128)} %bitcast.7, s32[1,32]{1,0:T(1,128)} %bitcast.8, bf16[512,512]{1,0:T(8,128)(2,1)} %constant.16.clone.refs_0_, bf16[1024,1024]{1,0:T(8,128)(2,1)} %constant.17.clone.refs_1_, ...), custom_call_target="tpu_custom_call" | custom-call | tf_op jit(solution)/shard_map/pallas_call | solution.py:635
  41.5 0.6 %broadcast_multiply_fusion = f32[64,128]{1,0:T(8,128)} fusion(f32[64,128]{1,0:T(8,128)S(1)} %shard_map.109), kind=kLoop, calls=%fused_computation | loop fusion | flops 8192 | bytes 65536 | tf_op jit(solution)/shard_map/mul | solution.py:674

commit v8 on v7

--- a/solution.py
+++ b/solution.py
@@ -312,12 +312,12 @@
         pltpu.make_async_copy(taps.at[me, :, share], tin.at[me, :, share], own_sem.at[1]),
     ]
     barrier = pltpu.get_barrier_semaphore()
+    for o in reversed(range(1, chan)):
+        pl.semaphore_signal(barrier, inc=1, device_id={"chan": partner(o)}, device_id_type=MESH)
     for o in range(1, hour):
         pl.semaphore_signal(
             barrier, inc=1, device_id={"hour": lax.rem(my_hour + o, hour)}, device_id_type=MESH
         )
-    for o in range(1, chan):
-        pl.semaphore_signal(barrier, inc=1, device_id={"chan": partner(o)}, device_id_type=MESH)
     for copy in own + loads:
         copy.start()
     place = lax.broadcasted_iota(jnp.int32, ids.shape, 1)

time: 42.3 us -> 42.3 us (level)
  no operation moved by 1% of the time
where the time goes in v8:
time: 42.3 us; the launch traced here: 42.1 us
  Pallas kernels  41.5 us (98%)
  other arithmetic  0.62 us (1%)
    pallas_call x1, Pallas kernels, split_body(): pl.pallas_call(functools.partial(kernel, chan, hour), out_shape=pltpu.VME...  41.5 us

profile of v8, /device:TPU:0, one launch (start us, length us, event | category | flops | bytes accessed | tf_op | source)
XLA Modules:
  0.0 42.1 jit_solution(5925524679490657315)
XLA Ops:
  0.0 41.5 %shard_map.109 = f32[64,128]{1,0:T(8,128)S(1)} custom-call(bf16[8,16,4096]{2,1,0:T(8,128)(2,1)} %bitcast.5, bf16[8,16,512]{2,1,0:T(8,128)(2,1)} %bitcast.6, s32[1,4]{1,0:T(1,128)} %bitcast.7, s32[1,32]{1,0:T(1,128)} %bitcast.8, bf16[512,512]{1,0:T(8,128)(2,1)} %constant.16.clone.refs_0_, bf16[1024,1024]{1,0:T(8,128)(2,1)} %constant.17.clone.refs_1_, ...), custom_call_target="tpu_custom_call" | custom-call | tf_op jit(solution)/shard_map/pallas_call | solution.py:635
  41.5 0.6 %broadcast_multiply_fusion = f32[64,128]{1,0:T(8,128)} fusion(f32[64,128]{1,0:T(8,128)S(1)} %shard_map.109), kind=kLoop, calls=%fused_computation | loop fusion | flops 8192 | bytes 65536 | tf_op jit(solution)/shard_map/mul | solution.py:674
